TPU v7x, 32 devices: a whole 2x2x4 slice. The times are simulated.
32 devices in a mesh: dp: 4 (over y, x), fsdp: 8 (over z, core).
Axes of the slice: x: 2, y: 2, z: 4, core: 2. Of those that a mesh axis runs over, the one named last changes fastest.
Arguments:
- states: bfloat16 [8192, 8192], P(('dp', 'fsdp')), may hold values from -6 to 6
- queries: bfloat16 [8192, 4096], P(('dp', 'fsdp')), may hold values from -5 to 5
- keys: bfloat16 [8192, 1024], P(('dp', 'fsdp')), may hold values from -5 to 5
- dest_device: int32 [8192], P(('dp', 'fsdp')), may hold values from 0 to 31, as said below
- dest_offset: int32 [8192], P(('dp', 'fsdp')), may hold values from 0 to 255, as said below
- response_numbers: int32 [8192], P(('dp', 'fsdp')), may hold values from 0 to 3, as said below
- cotangent: bfloat16 [8192, 4096], P(('dp', 'fsdp')), may hold values from -6 to 6
- value_matrix: bfloat16 [8192, 1024], P('fsdp'), may hold values from -0.0625 to 0.0625
Outputs:
- attn_out: bfloat16 [8192, 4096], P(('dp', 'fsdp'))
- grad_query: bfloat16 [8192, 4096], P(('dp', 'fsdp'))
- grad_key: bfloat16 [8192, 1024], P(('dp', 'fsdp'))
- grad_value_weight: float32 [8192, 1024], P('fsdp')
Inputs may be any that keep to these rules, and one draw needn't show every extreme that they name: `dest_device`: each device sends exactly 8 rows to each of 32 different devices, and every device receives exactly 256 rows. `dest_offset`: the rows that one device receives have different offsets. `response_numbers`: each device's 256 rows hold exactly 4 responses in order: ids start at 0 on each device and never fall along its rows.
All inputs are finite; a program needn't handle non-finite values.
Results may differ from a plain program's by a relative error of at most 0.017.
Values may be sent and summed in bfloat16 or wider, within the bound.
A program may use at most 192 MiB of HBM per device.

v0:
```python
import math

import jax
import jax.numpy as jnp
from jax import lax
from jax.sharding import PartitionSpec as P

KEY_VALUE_HEADS = 8
HEAD_SIZE = 128
QUERY_HEADS = 32


def attend_block(
    block_query_rows, block_key_rows, block_value_rows, block_segments, block_upstream_grad
):
    token_count = block_query_rows.shape[0]
    head_group = QUERY_HEADS // KEY_VALUE_HEADS
    inverse = 1.0 / math.sqrt(HEAD_SIZE)
    query_head_rows = block_query_rows.reshape(token_count, KEY_VALUE_HEADS, head_group, HEAD_SIZE)
    key_head_rows = block_key_rows.reshape(token_count, KEY_VALUE_HEADS, HEAD_SIZE)
    value_head_rows = block_value_rows.reshape(token_count, KEY_VALUE_HEADS, HEAD_SIZE)
    output_gradient = block_upstream_grad.reshape(
        token_count, KEY_VALUE_HEADS, head_group, HEAD_SIZE
    )
    scores = (
        jnp.einsum(
            "tkgd,skd->kgts", query_head_rows, key_head_rows, preferred_element_type=jnp.float32
        )
        * inverse
    )
    position = jnp.arange(token_count, dtype=jnp.int32)
    allowed = (position[None, :] <= position[:, None]) & (
        block_segments[None, :] == block_segments[:, None]
    )
    scores = jnp.where(allowed, scores, -1e30)
    highest = jnp.max(scores, axis=-1, keepdims=True)
    expon = jnp.exp(scores - highest)
    probs = expon / jnp.sum(expon, axis=-1, keepdims=True)
    probs_low = probs.astype(jnp.bfloat16)
    attention_fn = jnp.einsum(
        "kgts,skd->tkgd", probs_low, value_head_rows, preferred_element_type=jnp.float32
    ).astype(jnp.bfloat16)
    dprobs = jnp.einsum(
        "tkgd,skd->kgts", output_gradient, value_head_rows, preferred_element_type=jnp.float32
    )
    delta = jnp.sum(probs * dprobs, axis=-1, keepdims=True)
    dscores = (probs * (dprobs - delta)).astype(jnp.bfloat16)
    query_gradient = (
        jnp.einsum("kgts,skd->tkgd", dscores, key_head_rows, preferred_element_type=jnp.float32)
        * inverse
    ).astype(jnp.bfloat16)
    key_gradient = (
        jnp.einsum("kgts,tkgd->skd", dscores, query_head_rows, preferred_element_type=jnp.float32)
        * inverse
    ).astype(jnp.bfloat16)
    value_gradient = jnp.einsum(
        "kgts,tkgd->skd", probs_low, output_gradient, preferred_element_type=jnp.float32
    ).astype(jnp.bfloat16)
    return (
        attention_fn.reshape(token_count, QUERY_HEADS * HEAD_SIZE),
        query_gradient.reshape(token_count, QUERY_HEADS * HEAD_SIZE),
        key_gradient.reshape(token_count, KEY_VALUE_HEADS * HEAD_SIZE),
        value_gradient.reshape(token_count, KEY_VALUE_HEADS * HEAD_SIZE),
    )


def ordered_dot(one_hot, rows):
    return jnp.dot(one_hot, rows, preferred_element_type=jnp.float32).astype(rows.dtype)


def per_device(
    states, queries, keys, dest_device, dest_offset, response_numbers, cotangent, value_matrix
):
    token_count, model_width = states.shape
    group_dp = lax.axis_size("dp")
    group_fsdp = lax.axis_size("fsdp")
    device_count = group_dp * group_fsdp
    capacity = token_count // device_count
    everyone = ("dp", "fsdp")
    low = states.dtype
    share = value_matrix.shape[0] // group_dp
    own_share = lax.dynamic_slice_in_dim(value_matrix, lax.axis_index("dp") * share, share, 0)
    whole = lax.all_gather(own_share, everyone, axis=0)

    row = jnp.arange(token_count, dtype=jnp.int32)
    earlier = (dest_device[:, None] == dest_device[None, :]) & (row[None, :] < row[:, None])
    slot = jnp.sum(earlier.astype(jnp.int32), axis=1)
    index = dest_device * capacity + slot
    pack = (index[None, :] == row[:, None]).astype(low)
    tail = jnp.broadcast_to(dest_offset.astype(low)[:, None], (token_count, 128))
    joined = jnp.concatenate([queries, keys, tail], axis=1)

    def exchange(rows):
        width = rows.shape[1]
        moved = lax.all_to_all(
            rows.reshape(device_count, capacity, width),
            everyone,
            split_axis=0,
            concat_axis=0,
            tiled=True,
        )
        return moved.reshape(token_count, width)

    got = exchange(ordered_dot(pack, joined))
    whole = whole.reshape(group_dp, group_fsdp, share, -1).transpose(1, 0, 2, 3)
    whole = whole.reshape(model_width, -1)
    values = jnp.dot(states, whole, preferred_element_type=jnp.float32).astype(low)
    got_values = exchange(ordered_dot(pack, values))
    target = got[:, -128].astype(jnp.int32)
    place = (target[None, :] == row[:, None]).astype(low)
    query_width = queries.shape[1]
    placed = ordered_dot(place, got)
    learner_queries = placed[:, :query_width]
    learner_keys = placed[:, query_width : query_width + keys.shape[1]]
    attention_fn, query_gradient, key_gradient, value_gradient = attend_block(
        learner_queries, learner_keys, ordered_dot(place, got_values), response_numbers, cotangent
    )
    returned = exchange(ordered_dot(place.T, value_gradient))
    row_grads = ordered_dot(pack.T, returned)
    term = lax.dot_general(
        states, row_grads, (((0,), (0,)), ((), ())), preferred_element_type=jnp.float32
    ).astype(low)
    width = term.shape[1]
    term = term.reshape(group_fsdp, group_dp, share, width).transpose(1, 0, 2, 3)
    term = term.reshape(model_width, width)
    owned = lax.psum_scatter(term, everyone, scatter_dimension=0, tiled=True)
    summed = lax.all_gather(owned, "dp", axis=0, tiled=True).astype(jnp.float32)
    score_scale = 1.0 / math.sqrt(token_count * device_count)
    return (attention_fn, query_gradient, key_gradient, summed * score_scale)


def solution(mesh):
    in_specs = (
        P(("dp", "fsdp"), None),
        P(("dp", "fsdp"), None),
        P(("dp", "fsdp"), None),
        P(("dp", "fsdp")),
        P(("dp", "fsdp")),
        P(("dp", "fsdp")),
        P(("dp", "fsdp"), None),
        P("fsdp", None),
    )
    out_specs = (
        P(("dp", "fsdp"), None),
        P(("dp", "fsdp"), None),
        P(("dp", "fsdp"), None),
        P("fsdp", None),
    )
    return jax.shard_map(
        per_device, mesh=mesh, in_specs=in_specs, out_specs=out_specs, check_vma=False
    )
```

profile of v0, /device:TPU:0, one launch (start us, length us, event | category | flops | bytes accessed | tf_op | source)
XLA Modules:
  0.0 478.4 jit_solution(6254969145576294509)
XLA Ops:
  12.0 4.2 fusion.4
  16.2 7.4 %all-to-all-start = ((bf16[32,8,5248]{2,1,0:T(8,128)(2,1)}), bf16[32,8,5248]{2,1,0:T(8,128)(2,1)}, u32[]{:S(2)}, u32[]{:S(2)}) async-start(bf16[32,8,5248]{2,1,0:T(8,128)(2,1)} %fusion.4), calls=%async_computation | async-start | bytes 5373952 | tf_op jit(solution)/shard_map/all_to_all | solution.py:95
  23.7 2.5 copy.98
  26.3 94.0 %all-to-all-done = bf16[32,8,5248]{2,1,0:T(8,128)(2,1)} async-done(((bf16[32,8,5248]{2,1,0:T(8,128)(2,1)}), bf16[32,8,5248]{2,1,0:T(8,128)(2,1)}, u32[]{:S(2)}, u32[]{:S(2)}) %all-to-all-start) | async-done | bytes 2687008 | tf_op jit(solution)/shard_map/all_to_all | solution.py:95
  121.2 2.7 convolution_convert_fusion
  127.0 3.3 copy.97
  132.2 5.0 %fusion.55 = (f32[8,4,256]{2,1,0:T(4,128)S(1)}, f32[8,4,256,256]{2,3,1,0:T(8,128)}) fusion(pred[256,256]{0,1:T(8,128)(4,1)S(1)} %fusion.42, bf16[256,8,128,1]{0,2,3,1:T(8,128)(2,1)S(1)} %copy.83, bf16[256,8,4,128]{0,3,2,1:T(8,128)(2,1)S(1)} %bitcast.102), kind=kOutput, calls=%fused_computation.70 | convolution fusion | flops 545259776 | bytes 11108352 | tf_op jit(solution)/shard_map/sub | solution.py:37
  137.2 5.5 %fusion.26 = bf16[8,256,128]{1,2,0:T(8,128)(2,1)S(1)} fusion(bf16[256,8,4,128]{0,3,2,1:T(8,128)(2,1)} %bitcast.105, f32[8,4,256,256]{2,3,1,0:T(8,128)} %get-tuple-element.21, f32[8,4,256]{2,1,0:T(4,128)S(1)} %get-tuple-element.20), kind=kOutput, calls=%fused_computation.33 | convolution fusion | flops 541327360 | bytes 11042816 | tf_op jit(solution)/shard_map/kgts,tkgd->skd/dot_general | solution.py:56
  143.1 29.1 %all_to_all.15 = bf16[32,8,1024]{2,1,0:T(8,128)(2,1)S(1)} all-to-all(bf16[32,8,1024]{2,1,0:T(8,128)(2,1)S(1)} %fusion.30), channel_id=1, replica_groups=mesh['dp'=4,'fsdp'=8] {'dp','fsdp'}, dimensions={0} | all-to-all | bytes 1048576 | tf_op jit(solution)/shard_map/all_to_all | solution.py:95
  172.2 10.7 %convert_bitcast_fusion = bf16[8192,1024]{0,1:T(8,128)(2,1)} fusion(bf16[256,8192]{1,0:T(8,128)(2,1)} %param.8, bf16[32,8,1024]{2,1,0:T(8,128)(2,1)S(1)} %all_to_all.15, s32[256]{0:T(256)S(1)} %multiply_add_fusion), kind=kOutput, calls=%fused_computation.1 | convolution fusion | flops 4437901312 | bytes 21496832 | tf_op jit(solution)/shard_map/dot_general | solution.py:120
  182.9 27.8 %reshape.94 = bf16[8,4,256,1024]{2,1,0,3:T(4,128)(2,1)} reshape(bf16[8192,1024]{0,1:T(8,128)(2,1)} %convert_bitcast_fusion) | data formatting | bytes 33554432 | tf_op jit(solution)/shard_map/reshape | solution.py:124
  210.7 26.1 %copy.75 = bf16[4,8,256,1024]{3,2,1,0:T(8,128)(2,1)} copy(bf16[4,8,256,1024]{2,0,1,3:T(4,128)(2,1)} %bitcast.99) | data formatting | bytes 33554432 | tf_op jit(solution)/shard_map/transpose | solution.py:124
  237.1 13.9 %copy.62 = bf16[8,4,256,1024]{3,2,1,0:T(8,128)(2,1)} copy(bf16[8,4,256,1024]{3,2,0,1:T(8,128)(2,1)} %bitcast.100) | data formatting | bytes 33554432 | tf_op jit(solution)/shard_map/transpose | solution.py:105
  251.1 12.1 %fusion.31 = bf16[32,8,1024]{2,1,0:T(8,128)(2,1)S(1)} fusion(bf16[8192,1024]{1,0:T(8,128)(2,1)} %bitcast.101, bf16[256,8192]{1,0:T(8,128)(2,1)} %param.8, s32[256]{0:T(256)S(1)} %multiply_add_fusion), kind=kOutput, calls=%fused_computation.41 | convolution fusion | flops 4429774848 | bytes 21496832 | tf_op jit(solution)/shard_map/dot_general | solution.py:68
  263.1 29.2 %all_to_all.16 = bf16[32,8,1024]{2,1,0:T(8,128)(2,1)S(1)} all-to-all(bf16[32,8,1024]{2,1,0:T(8,128)(2,1)S(1)} %fusion.31), channel_id=1, replica_groups=mesh['dp'=4,'fsdp'=8] {'dp','fsdp'}, dimensions={0} | all-to-all | bytes 1048576 | tf_op jit(solution)/shard_map/all_to_all | solution.py:95
  292.7 5.7 %fusion.18 = bf16[8,128,4,256]{3,1,2,0:T(8,128)(2,1)} fusion(bf16[256,8,128,1]{2,1,0,3:T(8,128)(2,1)S(1)} %bitcast.111, f32[8,4,256,256]{2,3,1,0:T(8,128)} %get-tuple-element.21, f32[8,4,256]{2,1,0:T(4,128)S(1)} %get-tuple-element.20), kind=kOutput, calls=%fused_computation.28 | convolution fusion | flops 542113792 | bytes 11042816 | tf_op jit(solution)/shard_map/kgts,skd->tkgd/dot_general | solution.py:40
  298.5 4.2 copy.76
  302.7 129.0 %reduce-scatter.2.cloned.1.call-done = bf16[256,1024]{1,0:T(8,128)(2,1)} async-done(((bf16[8192,1024]{1,0:T(8,128)(2,1)}), bf16[256,1024]{1,0:T(8,128)(2,1)}) %reduce-scatter.2.cloned.1.call-update) | async-done | bytes 524304 | tf_op jit(solution)/shard_map/reduce_scatter | solution.py:126
  431.7 4.2 fusion.1
  435.9 4.5 fusion.3
  443.2 2.9 copy.77
  446.1 4.5 fusion.25
  451.5 16.1 %all-gather.4.cloned.1.call-done = bf16[1024,1024]{1,0:T(8,128)(2,1)} async-done(((bf16[256,1024]{1,0:T(8,128)(2,1)}), bf16[1024,1024]{1,0:T(8,128)(2,1)}) %all-gather.4.cloned.1.call-update) | async-done | bytes 2097168 | tf_op jit(solution)/shard_map/all_gather | solution.py:127
  467.7 4.2 convert_multiply_fusion
  (39 shorter events, 15.8 us)
Async XLA Ops:
  7.2 1.6 copy-start
  7.2 229.9 %all-gather.6.cloned.1.call-start = ((), (), s32[]{:S(2)}) async-start(), calls=%async_computation.6 | async-start | bytes 17301504 | tf_op jit(solution)/shard_map/all_gather | solution.py:83
  16.2 7.5 %copy-start.5 = (bf16[256,4096]{1,0:T(8,128)(2,1)S(1)}, bf16[256,4096]{1,0:T(8,128)(2,1)}, u32[]{:S(2)}) copy-start(bf16[256,4096]{1,0:T(8,128)(2,1)} %param.14) | copy-start | bytes 6291460
  16.2 10.0 %copy-start.7 = (s32[256]{0:T(256)S(1)}, s32[256]{0:T(256)}, u32[]{:S(2)}) copy-start(s32[256]{0:T(256)} %param.13) | copy-start | bytes 3076
  16.2 104.1 %all-to-all-start = ((bf16[32,8,5248]{2,1,0:T(8,128)(2,1)}), bf16[32,8,5248]{2,1,0:T(8,128)(2,1)}, u32[]{:S(2)}, u32[]{:S(2)}) async-start(bf16[32,8,5248]{2,1,0:T(8,128)(2,1)} %fusion.4), calls=%async_computation | async-start | bytes 5373952 | tf_op jit(solution)/shard_map/all_to_all | solution.py:95
  23.6 408.0 %reduce-scatter.2.cloned.1.call-start = ((), (), s32[]{:S(2)}) async-start(), calls=%async_computation.4 | async-start | bytes 17301504 | tf_op jit(solution)/shard_map/reduce_scatter | solution.py:126
  123.9 1.5 copy-start.3
  130.3 7.0 %copy-start.4 = (bf16[256,4096]{0,1:T(8,128)(2,1)}, bf16[256,4096]{0,1:T(8,128)(2,1)S(1)}, u32[]{:S(2)}) copy-start(bf16[256,4096]{0,1:T(8,128)(2,1)S(1)} %copy.97) | copy-start | bytes 6291460
  236.9 230.8 %all-gather.4.cloned.1.call-start = ((), (), s32[]{:S(2)}) async-start(), calls=%async_computation.5 | async-start | bytes 2621440 | tf_op jit(solution)/shard_map/all_gather | solution.py:127
  298.5 133.2 %copy-start.6 = (bf16[256,4096]{0,1:T(8,128)(2,1)S(1)}, bf16[256,4096]{0,1:T(8,128)(2,1)}, u32[]{:S(2)}) copy-start(bf16[256,4096]{0,1:T(8,128)(2,1)} %copy.98) | copy-start | bytes 6291460
  440.4 2.0 copy-start.2
  446.1 25.8 %copy-start.1 = (bf16[1024,1024]{1,0:T(8,128)(2,1)S(1)}, bf16[1024,1024]{1,0:T(8,128)(2,1)}, u32[]{:S(2)}) copy-start(bf16[1024,1024]{1,0:T(8,128)(2,1)} %param.15) | copy-start | bytes 6291460
Sparse Core Ops, SparseCore 0:
  11.6 166.3 all-gather.5
  237.0 194.6 reduce-scatter.1
  433.5 34.1 all-gather.3
where the time goes:
time: 480 us; the launch traced here: 478 us
  waiting for transfers between devices  239 us (50%)
  local copies, waits for them, and re-layouts  91.3 us (19%)
  blocking collectives  58.3 us (12%)
  matrix products  56 us (12%)
  between operations  13.9 us (3%)
  other arithmetic  12 us (2%)
  starting transfers between devices  7.72 us (2%)
    reduce_scatter x1, waiting for transfers between devices, per_device(): owned = lax.psum_scatter(term, everyone, scatter_dimension=0, tiled=True)  129 us
    all_to_all x1, waiting for transfers between devices, exchange(): lax.all_to_all(rows.reshape(device_count, capacity, width), everyone, spl...  94 us
    all_to_all x2, blocking collectives, exchange(): lax.all_to_all(rows.reshape(device_count, capacity, width), everyone, spl...  58.3 us
    reshape x1, local copies, waits for them, and re-layouts, per_device(): term.reshape(group_fsdp, group_dp, share, width).transpose(1, 0, 2, 3)  27.8 us
    transpose x1, local copies, waits for them, and re-layouts, per_device(): term.reshape(group_fsdp, group_dp, share, width).transpose(1, 0, 2, 3)  26.1 us
    dot_general x5, matrix products, ordered_dot(): jnp.dot(one_hot, rows, preferred_element_type=jnp.float32)  19.6 us
    all_gather x1, waiting for transfers between devices, per_device(): summed = lax.all_gather(owned, 'dp', axis=0, tiled=True).astype(jnp.float32)  16.1 us
    unnamed x22, local copies, waits for them, and re-layouts  14.8 us
  transfers between devices with their start and end apart: 4, of which 3 were waited for; matrix products, arithmetic and copies ran while one was open for 31% of the time, Pallas kernels for 0%

commit v1 on v0

v1 whole, which is shorter than its diff:
```python
import math

import jax
import jax.numpy as jnp
from jax import lax
from jax.experimental import pallas as pl
from jax.sharding import PartitionSpec as P

KEY_VALUE_HEADS = 8
HEAD_SIZE = 128
QUERY_HEADS = 32


def attend_kernel(q_ref, k_ref, v_ref, g_ref, col_ref, row_ref, o_ref, dq_ref, dk_ref, dv_ref):
    token_count = k_ref.shape[0]
    inverse = 1.0 / math.sqrt(HEAD_SIZE)
    low = q_ref.dtype
    query_at = lax.broadcasted_iota(jnp.int32, (token_count, token_count), 0)
    key_at = lax.broadcasted_iota(jnp.int32, (token_count, token_count), 1)
    allowed = (key_at <= query_at) & (row_ref[...] == col_ref[...])
    k = k_ref[...]
    v = v_ref[...]

    def dot(x, y, dims):
        return lax.dot_general(x, y, (dims, ((), ())), preferred_element_type=jnp.float32)

    for head in range(QUERY_HEADS // KEY_VALUE_HEADS):
        part = slice(head * HEAD_SIZE, (head + 1) * HEAD_SIZE)
        q = q_ref[:, part]
        g = g_ref[:, part]
        scores = jnp.where(allowed, dot(q, k, ((1,), (1,))) * inverse, -1e30)
        expon = jnp.exp(scores - jnp.max(scores, axis=1, keepdims=True))
        probs = expon * (1.0 / jnp.sum(expon, axis=1, keepdims=True))
        probs_low = probs.astype(low)
        o_ref[:, part] = dot(probs_low, v, ((1,), (0,))).astype(low)
        dprobs = dot(g, v, ((1,), (1,)))
        delta = jnp.sum(probs * dprobs, axis=1, keepdims=True)
        dscores = (probs * (dprobs - delta)).astype(low)
        dq_ref[:, part] = (dot(dscores, k, ((1,), (0,))) * inverse).astype(low)
        key_term = dot(dscores, q, ((0,), (0,)))
        value_term = dot(probs_low, g, ((0,), (0,)))
        dk = key_term if head == 0 else dk + key_term
        dv = value_term if head == 0 else dv + value_term
    dk_ref[...] = (dk * inverse).astype(low)
    dv_ref[...] = dv.astype(low)


def attend_block(q, k, v, segments, g):
    token_count = q.shape[0]
    wide = pl.BlockSpec((token_count, q.shape[1] // KEY_VALUE_HEADS), lambda h: (0, h))
    thin = pl.BlockSpec((token_count, HEAD_SIZE), lambda h: (0, h))
    col = pl.BlockSpec((token_count, 1), lambda h: (0, 0))
    row = pl.BlockSpec((1, token_count), lambda h: (0, 0))
    out = [jax.ShapeDtypeStruct(x.shape, q.dtype) for x in (q, q, k, k)]
    return pl.pallas_call(
        attend_kernel,
        grid=(KEY_VALUE_HEADS,),
        in_specs=[wide, thin, thin, wide, col, row],
        out_specs=[wide, wide, thin, thin],
        out_shape=out,
        cost_estimate=pl.CostEstimate(
            flops=12 * QUERY_HEADS * token_count * token_count * HEAD_SIZE,
            bytes_accessed=40 * token_count * QUERY_HEADS * HEAD_SIZE // 4,
            transcendentals=QUERY_HEADS * token_count * token_count,
        ),
    )(q, k, v, g, segments[:, None], segments[None, :])


def ordered_dot(one_hot, rows):
    return jnp.dot(one_hot, rows, preferred_element_type=jnp.float32).astype(rows.dtype)


def per_device(
    states, queries, keys, dest_device, dest_offset, response_numbers, cotangent, value_matrix
):
    token_count, model_width = states.shape
    group_dp = lax.axis_size("dp")
    group_fsdp = lax.axis_size("fsdp")
    device_count = group_dp * group_fsdp
    capacity = token_count // device_count
    everyone = ("dp", "fsdp")
    low = states.dtype
    share = value_matrix.shape[0] // group_dp
    own_share = lax.dynamic_slice_in_dim(value_matrix, lax.axis_index("dp") * share, share, 0)
    whole = lax.all_gather(own_share, everyone, axis=0)

    row = jnp.arange(token_count, dtype=jnp.int32)
    earlier = (dest_device[:, None] == dest_device[None, :]) & (row[None, :] < row[:, None])
    slot = jnp.sum(earlier.astype(jnp.int32), axis=1)
    index = dest_device * capacity + slot
    pack = (index[None, :] == row[:, None]).astype(low)
    tail = jnp.broadcast_to(dest_offset.astype(low)[:, None], (token_count, 128))
    joined = jnp.concatenate([queries, keys, tail], axis=1)

    def exchange(rows):
        width = rows.shape[1]
        moved = lax.all_to_all(
            rows.reshape(device_count, capacity, width),
            everyone,
            split_axis=0,
            concat_axis=0,
            tiled=True,
        )
        return moved.reshape(token_count, width)

    got = exchange(ordered_dot(pack, joined))
    whole = whole.reshape(group_dp, group_fsdp, share, -1).transpose(1, 0, 2, 3)
    whole = whole.reshape(model_width, -1)
    values = jnp.dot(states, whole, preferred_element_type=jnp.float32).astype(low)
    got_values = exchange(ordered_dot(pack, values))
    block = model_width // group_fsdp
    moving, got_values = lax.optimization_barrier((states, got_values))
    column_states = lax.all_to_all(
        moving.reshape(token_count, group_fsdp, block).transpose(1, 0, 2),
        "fsdp",
        split_axis=0,
        concat_axis=0,
        tiled=True,
    ).reshape(group_fsdp * token_count, block)
    target = got[:, -128].astype(jnp.int32)
    place = (target[None, :] == row[:, None]).astype(low)
    query_width = queries.shape[1]
    placed = ordered_dot(place, got)
    learner_queries = placed[:, :query_width]
    learner_keys = placed[:, query_width : query_width + keys.shape[1]]
    attention_fn, query_gradient, key_gradient, value_gradient = attend_block(
        learner_queries, learner_keys, ordered_dot(place, got_values), response_numbers, cotangent
    )
    returned = exchange(ordered_dot(place.T, value_gradient))
    row_grads = ordered_dot(pack.T, returned)
    group_grads = lax.all_gather(row_grads, "fsdp", axis=0, tiled=True)
    term = lax.dot_general(
        column_states, group_grads, (((0,), (0,)), ((), ())), preferred_element_type=jnp.float32
    ).astype(low)
    summed = lax.psum(term, "dp").astype(jnp.float32)
    score_scale = 1.0 / math.sqrt(token_count * device_count)
    return (attention_fn, query_gradient, key_gradient, summed * score_scale)


def solution(mesh):
    in_specs = (
        P(("dp", "fsdp"), None),
        P(("dp", "fsdp"), None),
        P(("dp", "fsdp"), None),
        P(("dp", "fsdp")),
        P(("dp", "fsdp")),
        P(("dp", "fsdp")),
        P(("dp", "fsdp"), None),
        P("fsdp", None),
    )
    out_specs = (
        P(("dp", "fsdp"), None),
        P(("dp", "fsdp"), None),
        P(("dp", "fsdp"), None),
        P("fsdp", None),
    )
    return jax.shard_map(
        per_device, mesh=mesh, in_specs=in_specs, out_specs=out_specs, check_vma=False
    )
```

time: 480 us -> 486 us (1.012)
  waiting for transfers between devices: 239 us -> 358 us
  local copies, waits for them, and re-layouts: 91.3 us -> 32.3 us
  blocking collectives: 58.3 us -> 0 us
  matrix products: 56 us -> 33.3 us
  Pallas kernels: 0 us -> 21.7 us
  starting transfers between devices: 7.72 us -> 17.7 us
    all_gather x1, waiting for transfers between devices: 0.02 us -> 146 us  [per_device(): whole = lax.all_gather(own_share, everyone, axis=0)]
    reduce_scatter x1 -> x0, waiting for transfers between devices: 129 us -> none  [per_device(): owned = lax.psum_scatter(term, everyone, scatter_dimension=0, tiled=True)]
    all_to_all x0 -> x1, waiting for transfers between devices: none -> 126 us  [per_device(): lax.all_to_all(moving.reshape(token_count, group_fsdp, block).transpose(1...]
    all_to_all x1 -> x3, waiting for transfers between devices: 94 us -> 19.5 us  [exchange(): lax.all_to_all(rows.reshape(device_count, capacity, width), everyone, spl...]
    psum x0 -> x1, waiting for transfers between devices: none -> 66.8 us  [per_device(): summed = lax.psum(term, 'dp').astype(jnp.float32)]
    all_to_all x2 -> x0, blocking collectives: 58.3 us -> none  [exchange(): lax.all_to_all(rows.reshape(device_count, capacity, width), everyone, spl...]
    reshape x4 -> x0, local copies, waits for them, and re-layouts: 33.9 us -> none  [the longest x1 27.8 us: per_device(): term.reshape(group_fsdp, group_dp, share, width).transpose(1, 0, 2, 3)]
    transpose x1 -> x0, local copies, waits for them, and re-layouts: 26.1 us -> none  [per_device(): term.reshape(group_fsdp, group_dp, share, width).transpose(1, 0, 2, 3)]
  transfers between devices with their start and end apart: 4 -> 7, of which waited for: 3 -> 5; matrix products, arithmetic and copies ran while one was open for 31% -> 11% of each run, Pallas kernels for 0% -> 0%
where the time goes in v1:
time: 486 us; the launch traced here: 485 us
  waiting for transfers between devices  358 us (74%)
  matrix products  33.3 us (7%)
  local copies, waits for them, and re-layouts  32.3 us (7%)
  Pallas kernels  21.7 us (4%)
  starting transfers between devices  17.7 us (4%)
  between operations  13.8 us (3%)
  other arithmetic  7.46 us (2%)
    all_gather x1, waiting for transfers between devices, per_device(): whole = lax.all_gather(own_share, everyone, axis=0)  146 us
    all_to_all x1, waiting for transfers between devices, per_device(): lax.all_to_all(moving.reshape(token_count, group_fsdp, block).transpose(1...  126 us
    psum x1, waiting for transfers between devices, per_device(): summed = lax.psum(term, 'dp').astype(jnp.float32)  66.8 us
    dot_general x6, matrix products, ordered_dot(): jnp.dot(one_hot, rows, preferred_element_type=jnp.float32)  23.9 us
    pallas_call x1, Pallas kernels, attend_block(): pl.pallas_call(attend_kernel, grid=(KEY_VALUE_HEADS,), in_specs=[wide, th...  21.7 us
    all_to_all x3, waiting for transfers between devices, exchange(): lax.all_to_all(rows.reshape(device_count, capacity, width), everyone, spl...  19.5 us
    transpose x1, local copies, waits for them, and re-layouts, per_device(): whole = whole.reshape(group_dp, group_fsdp, share, -1).transpose(1, 0, 2, 3)  13.8 us
    all_to_all x3, starting transfers between devices, exchange(): lax.all_to_all(rows.reshape(device_count, capacity, width), everyone, spl...  12.9 us
  transfers between devices with their start and end apart: 7, of which 5 were waited for; matrix products, arithmetic and copies ran while one was open for 11% of the time, Pallas kernels for 0%

profile of v1, /device:TPU:0, one launch (start us, length us, event | category | flops | bytes accessed | tf_op | source)
XLA Modules:
  0.0 484.5 jit_solution(11944787845437980310)
XLA Ops:
  7.2 1.5 copy-done
  12.0 4.2 fusion
  16.2 7.4 %all-to-all-start = ((bf16[32,8,5248]{2,1,0:T(8,128)(2,1)}), bf16[32,8,5248]{2,1,0:T(8,128)(2,1)}, u32[]{:S(2)}, u32[]{:S(2)}) async-start(bf16[32,8,5248]{2,1,0:T(8,128)(2,1)} %fusion), calls=%async_computation | async-start | bytes 5373952 | tf_op jit(solution)/shard_map/all_to_all | solution.py:97
  23.6 145.6 %all-gather.6.cloned.1.call-done = bf16[8192,1024]{1,0:T(8,128)(2,1)} async-done(((bf16[256,1024]{1,0:T(8,128)(2,1)}), bf16[8192,1024]{1,0:T(8,128)(2,1)}) %all-gather.6.cloned.1.call-update) | async-done | bytes 16777232 | tf_op jit(solution)/shard_map/all_gather | solution.py:85
  169.2 13.8 %copy.18 = bf16[8,4,256,1024]{3,2,1,0:T(8,128)(2,1)} copy(bf16[8,4,256,1024]{3,2,0,1:T(8,128)(2,1)} %bitcast.29) | data formatting | bytes 33554432 | tf_op jit(solution)/shard_map/transpose | solution.py:107
  183.1 12.6 %fusion.7 = bf16[32,8,1024]{2,1,0:T(8,128)(2,1)} fusion(bf16[8192,1024]{1,0:T(8,128)(2,1)} %bitcast.30, bf16[256,8192]{1,0:T(8,128)(2,1)} %param.8, s32[256]{0:T(256)S(1)} %multiply_add_fusion), kind=kOutput, calls=%fused_computation.16 | convolution fusion | flops 4429774848 | bytes 21496832 | tf_op jit(solution)/shard_map/dot_general | solution.py:70
  195.7 2.9 all-to-all-start.1
  199.4 1.0 convert_reduce_fusion.1
  200.3 2.6 convolution_convert_fusion
  203.0 1.6 slice.13.q_ref
  205.4 9.5 %all-to-all-done.1 = bf16[32,8,1024]{2,1,0:T(8,128)(2,1)S(1)} async-done(((bf16[32,8,1024]{2,1,0:T(8,128)(2,1)}), bf16[32,8,1024]{2,1,0:T(8,128)(2,1)S(1)}, u32[]{:S(2)}, u32[]{:S(2)}) %all-to-all-start.1) | async-done | bytes 524320 | tf_op jit(solution)/shard_map/all_to_all | solution.py:97
  214.9 1.1 convolution_convert_fusion.5.v_ref
  216.0 21.7 %shard_map.111 = (bf16[256,4096]{1,0:T(8,128)(2,1)}, bf16[256,4096]{1,0:T(8,128)(2,1)}, bf16[256,1024]{1,0:T(8,128)(2,1)}, bf16[256,1024]{1,0:T(8,128)(2,1)}) custom-call(bf16[256,4096]{1,0:T(8,128)(2,1)} %slice.13.q_ref, bf16[256,1024]{1,0:T(8,128)(2,1)} %slice.14.k_ref, bf16[256,1024]{1,0:T(8,128)(2,1)} %convolution_convert_fusion.5.v_ref, ...), custom_call_target="tpu_custom_call" | custom-call | flops 3221225472 | bytes 10485760 | tf_op jit(solution)/shard_map/pallas_call | solution.py:55
  237.7 2.2 fusion.6
  239.9 2.6 all-to-all-start.3
  242.5 6.4 %copy.20 = bf16[256,8192]{0,1:T(8,128)(2,1)} copy(bf16[256,8192]{1,0:T(8,128)(2,1)} %param.8) | data formatting | bytes 8388608 | tf_op jit(solution)/shard_map/optimization_barrier | solution.py:112
  248.9 10.0 %all-to-all-done.3 = bf16[32,8,1024]{2,1,0:T(8,128)(2,1)S(1)} async-done(((bf16[32,8,1024]{2,1,0:T(8,128)(2,1)}), bf16[32,8,1024]{2,1,0:T(8,128)(2,1)S(1)}, u32[]{:S(2)}, u32[]{:S(2)}) %all-to-all-start.3) | async-done | bytes 524320 | tf_op jit(solution)/shard_map/all_to_all | solution.py:97
  258.9 4.6 all-to-all-start.2
  263.5 1.2 convolution_convert_fusion.3
  264.9 126.2 %all-to-all-done.2 = bf16[8,256,1024]{1,2,0:T(8,128)(2,1)} async-done(((bf16[8,256,1024]{1,2,0:T(8,128)(2,1)}), bf16[8,256,1024]{1,2,0:T(8,128)(2,1)}, u32[]{:S(2)}, u32[]{:S(2)}) %all-to-all-start.2) | async-done | bytes 4194336 | tf_op jit(solution)/shard_map/all_to_all | solution.py:113
  391.2 6.4 %copy.21 = bf16[8,256,1024]{2,1,0:T(8,128)(2,1)} copy(bf16[8,256,1024]{1,2,0:T(8,128)(2,1)} %all-to-all-done.2) | data formatting | bytes 8388608 | tf_op jit(solution)/shard_map/all_to_all | solution.py:113
  397.6 9.4 %convolution_convert_fusion.2 = bf16[1024,1024]{1,0:T(8,128)(2,1)} fusion(bf16[2048,1024]{1,0:T(8,128)(2,1)} %bitcast.32, bf16[2048,1024]{1,0:T(8,128)(2,1)} %all-gather.4.cloned.1.call-done), kind=kOutput, calls=%fused_computation.9 | convolution fusion | flops 4296015872 | bytes 10485760 | tf_op jit(solution)/shard_map/dot_general | solution.py:132
  407.0 66.8 %all-reduce.2.cloned.1.call-done = bf16[1024,1024]{1,0:T(8,128)(2,1)} async-done(((bf16[1024,1024]{1,0:T(8,128)(2,1)}), bf16[1024,1024]{1,0:T(8,128)(2,1)}) %all-reduce.2.cloned.1.call-update) | async-done | bytes 2097168 | tf_op jit(solution)/shard_map/psum | solution.py:135
  473.8 4.2 convert_multiply_fusion
  (20 shorter events, 5.3 us)
Async XLA Ops:
  7.2 1.6 copy-start
  7.2 162.1 %all-gather.6.cloned.1.call-start = ((), (), s32[]{:S(2)}) async-start(), calls=%async_computation.6 | async-start | bytes 17301504 | tf_op jit(solution)/shard_map/all_gather | solution.py:85
  16.2 179.5 %all-to-all-start = ((bf16[32,8,5248]{2,1,0:T(8,128)(2,1)}), bf16[32,8,5248]{2,1,0:T(8,128)(2,1)}, u32[]{:S(2)}, u32[]{:S(2)}) async-start(bf16[32,8,5248]{2,1,0:T(8,128)(2,1)} %fusion), calls=%async_computation | async-start | bytes 5373952 | tf_op jit(solution)/shard_map/all_to_all | solution.py:97
  183.1 15.5 %copy-start.2 = (s32[256]{0:T(256)S(1)}, s32[256]{0:T(256)}, u32[]{:S(2)}) copy-start(s32[256]{0:T(256)} %param.13) | copy-start | bytes 3076
  195.7 19.2 %all-to-all-start.1 = ((bf16[32,8,1024]{2,1,0:T(8,128)(2,1)}), bf16[32,8,1024]{2,1,0:T(8,128)(2,1)S(1)}, u32[]{:S(2)}, u32[]{:S(2)}) async-start(bf16[32,8,1024]{2,1,0:T(8,128)(2,1)} %fusion.7), calls=%async_computation.1 | async-start | bytes 1048576 | tf_op jit(solution)/shard_map/all_to_all | solution.py:97
  239.9 19.0 %all-to-all-start.3 = ((bf16[32,8,1024]{2,1,0:T(8,128)(2,1)}), bf16[32,8,1024]{2,1,0:T(8,128)(2,1)S(1)}, u32[]{:S(2)}, u32[]{:S(2)}) async-start(bf16[32,8,1024]{2,1,0:T(8,128)(2,1)} %fusion.6), calls=%async_computation.3 | async-start | bytes 1048576 | tf_op jit(solution)/shard_map/all_to_all | solution.py:97
  258.9 132.3 %all-to-all-start.2 = ((bf16[8,256,1024]{1,2,0:T(8,128)(2,1)}), bf16[8,256,1024]{1,2,0:T(8,128)(2,1)}, u32[]{:S(2)}, u32[]{:S(2)}) async-start(bf16[8,256,1024]{1,2,0:T(8,128)(2,1)} %bitcast.31), calls=%async_computation.2 | async-start | bytes 8388608 | tf_op jit(solution)/shard_map/all_to_all | solution.py:113
  263.4 134.1 %all-gather.4.cloned.1.call-start = ((), (), s32[]{:S(2)}) async-start(), calls=%async_computation.4 | async-start | bytes 4718592 | tf_op jit(solution)/shard_map/all_gather | solution.py:131
  264.7 209.1 %all-reduce.2.cloned.1.call-start = ((), (), s32[]{:S(2)}) async-start(), calls=%async_computation.5 | async-start | bytes 4194304 | tf_op jit(solution)/shard_map/psum | solution.py:135
  407.0 71.0 %copy-start.1 = (bf16[1024,1024]{1,0:T(8,128)(2,1)S(1)}, bf16[1024,1024]{1,0:T(8,128)(2,1)}, u32[]{:S(2)}) copy-start(bf16[1024,1024]{1,0:T(8,128)(2,1)} %param.15) | copy-start | bytes 6291460
Sparse Core Ops, SparseCore 0:
  11.6 157.5 all-gather.5
  265.9 79.8 all-gather.3
  407.1 66.6 all-reduce.1

commit v2 on v1

--- a/solution.py
+++ b/solution.py
@@ -81,6 +81,16 @@
     everyone = ("dp", "fsdp")
     low = states.dtype
     share = value_matrix.shape[0] // group_dp
+    block = model_width // group_fsdp
+    me = lax.axis_index("fsdp")
+    blocks = []
+    for step in range(group_fsdp):
+        to = lax.rem(me + step, group_fsdp)
+        piece = lax.dynamic_slice_in_dim(states, to * block, block, 1)
+        if step:
+            pairs = [(i, (i + step) % group_fsdp) for i in range(group_fsdp)]
+            piece = lax.ppermute(piece, "fsdp", pairs)
+        blocks.append(piece)
     own_share = lax.dynamic_slice_in_dim(value_matrix, lax.axis_index("dp") * share, share, 0)
     whole = lax.all_gather(own_share, everyone, axis=0)
 
@@ -104,19 +114,10 @@
         return moved.reshape(token_count, width)
 
     got = exchange(ordered_dot(pack, joined))
-    whole = whole.reshape(group_dp, group_fsdp, share, -1).transpose(1, 0, 2, 3)
-    whole = whole.reshape(model_width, -1)
-    values = jnp.dot(states, whole, preferred_element_type=jnp.float32).astype(low)
+    turned = states.reshape(token_count, group_fsdp, group_dp, share).transpose(0, 2, 1, 3)
+    turned = turned.reshape(token_count, model_width)
+    values = jnp.dot(turned, whole.reshape(model_width, -1), preferred_element_type=jnp.float32).astype(low)
     got_values = exchange(ordered_dot(pack, values))
-    block = model_width // group_fsdp
-    moving, got_values = lax.optimization_barrier((states, got_values))
-    column_states = lax.all_to_all(
-        moving.reshape(token_count, group_fsdp, block).transpose(1, 0, 2),
-        "fsdp",
-        split_axis=0,
-        concat_axis=0,
-        tiled=True,
-    ).reshape(group_fsdp * token_count, block)
     target = got[:, -128].astype(jnp.int32)
     place = (target[None, :] == row[:, None]).astype(low)
     query_width = queries.shape[1]
@@ -126,15 +127,39 @@
     attention_fn, query_gradient, key_gradient, value_gradient = attend_block(
         learner_queries, learner_keys, ordered_dot(place, got_values), response_numbers, cotangent
     )
+    back = [blocks[-t % group_fsdp] for t in range(group_fsdp)]
+    first = lax.rem(group_fsdp - me, group_fsdp) * token_count
+    column_states = lax.dynamic_slice_in_dim(
+        jnp.concatenate(back + back[:-1], axis=0), first, group_fsdp * token_count, 0
+    )
+    value_gradient, column_states = lax.optimization_barrier((value_gradient, column_states))
     returned = exchange(ordered_dot(place.T, value_gradient))
     row_grads = ordered_dot(pack.T, returned)
     group_grads = lax.all_gather(row_grads, "fsdp", axis=0, tiled=True)
     term = lax.dot_general(
         column_states, group_grads, (((0,), (0,)), ((), ())), preferred_element_type=jnp.float32
     ).astype(low)
-    summed = lax.psum(term, "dp").astype(jnp.float32)
     score_scale = 1.0 / math.sqrt(token_count * device_count)
-    return (attention_fn, query_gradient, key_gradient, summed * score_scale)
+    dp = lax.axis_index("dp")
+    rows = term.shape[0] // group_dp
+    rings = [[(i, (i + step) % group_dp) for i in range(group_dp)] for step in range(group_dp)]
+    summed = lax.dynamic_slice_in_dim(term, dp * rows, rows, 0).astype(jnp.float32)
+    sent = []
+    for step in range(1, group_dp):
+        to = lax.rem(dp + step, group_dp)
+        piece = lax.dynamic_slice_in_dim(term, to * rows, rows, 0)
+        sent.append(lax.ppermute(piece, "dp", rings[step]))
+    for piece in sent:
+        summed = summed + piece.astype(jnp.float32)
+    summed = summed.astype(low)
+    weight_gradient = jnp.zeros(term.shape, jnp.float32)
+    for step in range(group_dp):
+        piece = lax.ppermute(summed, "dp", rings[step]) if step else summed
+        source = lax.rem(dp + group_dp - step, group_dp)
+        weight_gradient = lax.dynamic_update_slice_in_dim(
+            weight_gradient, piece.astype(jnp.float32) * score_scale, source * rows, 0
+        )
+    return (attention_fn, query_gradient, key_gradient, weight_gradient)
 
 
 def solution(mesh):

time: 486 us -> 456 us (0.938)
  waiting for transfers between devices: 358 us -> 240 us
  starting transfers between devices: 17.7 us -> 82.1 us
  blocking collectives: 0 us -> 18.4 us
  local copies, waits for them, and re-layouts: 32.3 us -> 41.8 us
    ppermute x0 -> x13, waiting for transfers between devices: none -> 191 us  [the longest x7 147 us: per_device(): piece = lax.ppermute(piece, 'fsdp', pairs)]
    all_gather x1, waiting for transfers between devices: 146 us -> 0.01 us  [per_device(): whole = lax.all_gather(own_share, everyone, axis=0)]
    all_to_all x1 -> x0, waiting for transfers between devices: 126 us -> none  [per_device(): lax.all_to_all(moving.reshape(token_count, group_fsdp, block).transpose(1...]
    ppermute x0 -> x13, starting transfers between devices: none -> 71.7 us  [the longest x7 64.7 us: per_device(): piece = lax.ppermute(piece, 'fsdp', pairs)]
    psum x1 -> x0, waiting for transfers between devices: 66.8 us -> none  [per_device(): summed = lax.psum(term, 'dp').astype(jnp.float32)]
    all_gather x1, waiting for transfers between devices: 0.01 us -> 44.9 us  [per_device(): group_grads = lax.all_gather(row_grads, 'fsdp', axis=0, tiled=True)]
    unnamed x6 -> x24, local copies, waits for them, and re-layouts: 1.55 us -> 21.8 us
    all_to_all x0 -> x1, blocking collectives: none -> 18.4 us  [exchange(): lax.all_to_all(rows.reshape(device_count, capacity, width), everyone, spl...]
  transfers between devices with their start and end apart: 7 -> 17, of which waited for: 5 -> 9; matrix products, arithmetic and copies ran while one was open for 11% -> 13% of each run, Pallas kernels for 0% -> 0%
where the time goes in v2:
time: 456 us; the launch traced here: 455 us
  waiting for transfers between devices  240 us (53%)
  starting transfers between devices  82.1 us (18%)
  local copies, waits for them, and re-layouts  41.8 us (9%)
  matrix products  31.1 us (7%)
  Pallas kernels  21.7 us (5%)
  blocking collectives  18.4 us (4%)
  between operations  14.3 us (3%)
  other arithmetic  5.65 us (1%)
    ppermute x7, waiting for transfers between devices, per_device(): piece = lax.ppermute(piece, 'fsdp', pairs)  147 us
    ppermute x7, starting transfers between devices, per_device(): piece = lax.ppermute(piece, 'fsdp', pairs)  64.7 us
    all_gather x1, waiting for transfers between devices, per_device(): group_grads = lax.all_gather(row_grads, 'fsdp', axis=0, tiled=True)  44.9 us
    ppermute x3, waiting for transfers between devices, per_device(): sent.append(lax.ppermute(piece, 'dp', rings[step]))  24 us
    dot_general x6, matrix products, ordered_dot(): jnp.dot(one_hot, rows, preferred_element_type=jnp.float32)  23 us
    unnamed x24, local copies, waits for them, and re-layouts  21.8 us
    pallas_call x1, Pallas kernels, attend_block(): pl.pallas_call(attend_kernel, grid=(KEY_VALUE_HEADS,), in_specs=[wide, th...  21.7 us
    ppermute x3, waiting for transfers between devices, per_device(): piece = lax.ppermute(summed, 'dp', rings[step]) if step else summed  20.8 us
  transfers between devices with their start and end apart: 17, of which 9 were waited for; matrix products, arithmetic and copies ran while one was open for 13% of the time, Pallas kernels for 0%

profile of v2, /device:TPU:0, one launch (start us, length us, event | category | flops | bytes accessed | tf_op | source)
XLA Modules:
  0.0 455.1 jit_solution(14924293075669057465)
XLA Ops:
  12.0 4.2 fusion
  16.2 7.4 %all-to-all-start = ((bf16[32,8,5248]{2,1,0:T(8,128)(2,1)}), bf16[32,8,5248]{2,1,0:T(8,128)(2,1)}, u32[]{:S(2)}, u32[]{:S(2)}) async-start(bf16[32,8,5248]{2,1,0:T(8,128)(2,1)} %fusion), calls=%async_computation | async-start | bytes 5373952 | tf_op jit(solution)/shard_map/all_to_all | solution.py:107
  23.6 4.1 constant_dynamic-slice_fusion.4
  27.8 3.3 collective-permute-start
  31.6 2.5 collective-permute-start.3
  34.1 6.4 %copy.17 = bf16[256,8192]{0,1:T(8,128)(2,1)} copy(bf16[256,8192]{1,0:T(8,128)(2,1)} %param.8) | data formatting | bytes 8388608 | tf_op args[0]
  40.5 4.6 %copy.18 = bf16[256,4,8,256]{0,3,2,1:T(8,128)(2,1)} copy(bf16[256,4,8,256]{0,3,1,2:T(8,128)(2,1)} %bitcast.26) | data formatting | bytes 8388608 | tf_op jit(solution)/shard_map/transpose | solution.py:117
  45.9 66.1 %collective-permute-done = bf16[256,1024]{1,0:T(8,128)(2,1)S(1)} collective-permute-done((bf16[256,1024]{1,0:T(8,128)(2,1)S(1)}, bf16[256,1024]{1,0:T(8,128)(2,1)S(1)}, u32[]{:S(2)}, u32[]{:S(2)}) %collective-permute-start) | collective-permute-done | bytes 524320 | tf_op jit(solution)/shard_map/ppermute | solution.py:92
  112.9 12.6 %collective-permute-done.1 = bf16[256,1024]{1,0:T(8,128)(2,1)S(1)} collective-permute-done((bf16[256,1024]{1,0:T(8,128)(2,1)}, bf16[256,1024]{1,0:T(8,128)(2,1)S(1)}, u32[]{:S(2)}, u32[]{:S(2)}) %collective-permute-start.1) | collective-permute-done | bytes 524320 | tf_op jit(solution)/shard_map/ppermute | solution.py:92
  125.4 58.3 %collective-permute-start.6 = (bf16[256,1024]{1,0:T(8,128)(2,1)}, bf16[256,1024]{1,0:T(8,128)(2,1)S(1)}, u32[]{:S(2)}, u32[]{:S(2)}) collective-permute-start(bf16[256,1024]{1,0:T(8,128)(2,1)} %get-tuple-element.18), channel_id=1, source_target_pairs={{0,1},{1,2},{2,3},{3,4},{4,5},{5,6},{6,7},{7,0},{8,9},{9,10},{10,1... | collective-permute-start | bytes 1572872 | tf_op jit(solution)/shard_map/ppermute | solution.py:92
  185.5 67.8 %collective-permute-done.3 = bf16[256,1024]{1,0:T(8,128)(2,1)S(1)} collective-permute-done((bf16[256,1024]{1,0:T(8,128)(2,1)}, bf16[256,1024]{1,0:T(8,128)(2,1)S(1)}, u32[]{:S(2)}, u32[]{:S(2)}) %collective-permute-start.3) | collective-permute-done | bytes 524320 | tf_op jit(solution)/shard_map/ppermute | solution.py:92
  261.8 12.6 %fusion.7 = bf16[32,8,1024]{2,1,0:T(8,128)(2,1)} fusion(bf16[8192,1024]{1,0:T(8,128)(2,1)} %all-gather.6.cloned.1.call-done, bf16[256,8192]{0,1:T(8,128)(2,1)} %bitcast.27, s32[256]{0:T(256)S(1)} %multiply_add_fusion), kind=kOutput, calls=%fused_computation.15 | convolution fusion | flops 4429774848 | bytes 21496832 | tf_op jit(solution)/shard_map/dot_general | solution.py:70
  274.4 2.7 all-to-all-start.1
  279.0 4.6 %constant_dynamic-slice_fusion.3 = bf16[2048,1024]{1,0:T(8,128)(2,1)} fusion(bf16[3840,1024]{1,0:T(8,128)(2,1)} %constant_dynamic-update-slice_fusion, s32[]{:T(128)S(6)} %select_n.55), kind=kLoop, calls=%fused_computation.53 | loop fusion | bytes 8388612 | tf_op jit(solution)/shard_map/dynamic_slice | solution.py:132
  284.6 2.6 convolution_convert_fusion
  289.7 3.8 all-to-all-done.1
  294.6 21.7 %shard_map.111 = (bf16[256,4096]{1,0:T(8,128)(2,1)}, bf16[256,4096]{1,0:T(8,128)(2,1)}, bf16[256,1024]{1,0:T(8,128)(2,1)}, bf16[256,1024]{1,0:T(8,128)(2,1)}) custom-call(bf16[256,4096]{1,0:T(8,128)(2,1)} %slice.13.q_ref, bf16[256,1024]{1,0:T(8,128)(2,1)} %slice.14.k_ref, bf16[256,1024]{1,0:T(8,128)(2,1)} %convolution_convert_fusion.5.v_ref, ...), custom_call_target="tpu_custom_call" | custom-call | flops 3221225472 | bytes 10485760 | tf_op jit(solution)/shard_map/pallas_call | solution.py:55
  317.7 18.4 %all_to_all.15 = bf16[32,8,1024]{2,1,0:T(8,128)(2,1)S(1)} all-to-all(bf16[32,8,1024]{2,1,0:T(8,128)(2,1)S(1)} %fusion.6), channel_id=1, replica_groups=mesh['dp'=4,'fsdp'=8] {'dp','fsdp'}, dimensions={0} | all-to-all | bytes 1048576 | tf_op jit(solution)/shard_map/all_to_all | solution.py:107
  337.3 44.9 %all-gather.4.cloned.1.call-done = bf16[2048,1024]{1,0:T(8,128)(2,1)} async-done(((bf16[256,1024]{1,0:T(8,128)(2,1)}), bf16[2048,1024]{1,0:T(8,128)(2,1)}) %all-gather.4.cloned.1.call-update) | async-done | bytes 4194320 | tf_op jit(solution)/shard_map/all_gather | solution.py:138
  382.2 8.0 %convolution_convert_fusion.2 = bf16[1024,1024]{1,0:T(8,128)(2,1)S(1)} fusion(bf16[2048,1024]{1,0:T(8,128)(2,1)} %constant_dynamic-slice_fusion.3, bf16[2048,1024]{1,0:T(8,128)(2,1)} %all-gather.4.cloned.1.call-done), kind=kOutput, calls=%fused_computation.8 | convolution fusion | flops 4296015872 | bytes 10485760 | tf_op jit(solution)/shard_map/dot_general | solution.py:139
  394.9 11.6 %collective-permute-done.9 = bf16[256,1024]{1,0:T(8,128)(2,1)} collective-permute-done((bf16[256,1024]{1,0:T(8,128)(2,1)}, bf16[256,1024]{1,0:T(8,128)(2,1)}, u32[]{:S(2)}, u32[]{:S(2)}) %collective-permute-start.9) | collective-permute-done | bytes 524320 | tf_op jit(solution)/shard_map/ppermute | solution.py:151
  406.5 12.4 %collective-permute-done.8 = bf16[256,1024]{1,0:T(8,128)(2,1)} collective-permute-done((bf16[256,1024]{1,0:T(8,128)(2,1)S(1)}, bf16[256,1024]{1,0:T(8,128)(2,1)}, u32[]{:S(2)}, u32[]{:S(2)}) %collective-permute-start.8) | collective-permute-done | bytes 524320 | tf_op jit(solution)/shard_map/ppermute | solution.py:151
  425.0 12.3 %collective-permute-done.10 = bf16[256,1024]{1,0:T(8,128)(2,1)S(1)} collective-permute-done((bf16[256,1024]{1,0:T(8,128)(2,1)S(1)}, bf16[256,1024]{1,0:T(8,128)(2,1)S(1)}, u32[]{:S(2)}, u32[]{:S(2)}) %collective-permute-start.10) | collective-permute-done | bytes 524320 | tf_op jit(solution)/shard_map/ppermute | solution.py:157
  437.4 8.6 %collective-permute-done.11 = bf16[256,1024]{1,0:T(8,128)(2,1)S(1)} collective-permute-done((bf16[256,1024]{1,0:T(8,128)(2,1)S(1)}, bf16[256,1024]{1,0:T(8,128)(2,1)S(1)}, u32[]{:S(2)}, u32[]{:S(2)}) %collective-permute-start.11) | collective-permute-done | bytes 524320 | tf_op jit(solution)/shard_map/ppermute | solution.py:157
  (64 shorter events, 39.2 us)
Async XLA Ops:
  7.2 1.6 copy-start
  7.2 254.6 %all-gather.6.cloned.1.call-start = ((), (), s32[]{:S(2)}) async-start(), calls=%async_computation.4 | async-start | bytes 17301504 | tf_op jit(solution)/shard_map/all_gather | solution.py:95
  16.2 258.2 %all-to-all-start = ((bf16[32,8,5248]{2,1,0:T(8,128)(2,1)}), bf16[32,8,5248]{2,1,0:T(8,128)(2,1)}, u32[]{:S(2)}, u32[]{:S(2)}) async-start(bf16[32,8,5248]{2,1,0:T(8,128)(2,1)} %fusion), calls=%async_computation | async-start | bytes 5373952 | tf_op jit(solution)/shard_map/all_to_all | solution.py:107
  27.8 84.3 %collective-permute-start = (bf16[256,1024]{1,0:T(8,128)(2,1)S(1)}, bf16[256,1024]{1,0:T(8,128)(2,1)S(1)}, u32[]{:S(2)}, u32[]{:S(2)}) collective-permute-start(bf16[256,1024]{1,0:T(8,128)(2,1)S(1)} %get-tuple-element.24), channel_id=1, source_target_pairs={{0,7},{1,0},{2,1},{3,2},{4,3},{5,4},{6,5},{7,6},{8,15},{9,8},{10,9... | collective-permute-start | bytes 1572872 | tf_op jit(solution)/shard_map/ppermute | solution.py:92
  31.1 94.3 %collective-permute-start.1 = (bf16[256,1024]{1,0:T(8,128)(2,1)}, bf16[256,1024]{1,0:T(8,128)(2,1)S(1)}, u32[]{:S(2)}, u32[]{:S(2)}) collective-permute-start(bf16[256,1024]{1,0:T(8,128)(2,1)} %get-tuple-element.23), channel_id=1, source_target_pairs={{0,6},{1,7},{2,0},{3,1},{4,2},{5,3},{6,4},{7,5},{8,14},{9,15},{10,... | collective-permute-start | bytes 1572872 | tf_op jit(solution)/shard_map/ppermute | solution.py:92
  31.6 153.0 %collective-permute-start.2 = (bf16[256,1024]{1,0:T(8,128)(2,1)}, bf16[256,1024]{1,0:T(8,128)(2,1)S(1)}, u32[]{:S(2)}, u32[]{:S(2)}) collective-permute-start(bf16[256,1024]{1,0:T(8,128)(2,1)} %get-tuple-element.22), channel_id=1, source_target_pairs={{0,5},{1,6},{2,7},{3,0},{4,1},{5,2},{6,3},{7,4},{8,13},{9,14},{10,... | collective-permute-start | bytes 1572872 | tf_op jit(solution)/shard_map/ppermute | solution.py:92
  31.6 221.6 %collective-permute-start.3 = (bf16[256,1024]{1,0:T(8,128)(2,1)}, bf16[256,1024]{1,0:T(8,128)(2,1)S(1)}, u32[]{:S(2)}, u32[]{:S(2)}) collective-permute-start(bf16[256,1024]{1,0:T(8,128)(2,1)} %get-tuple-element.21), channel_id=1, source_target_pairs={{0,4},{1,5},{2,6},{3,7},{4,0},{5,1},{6,2},{7,3},{8,12},{9,13},{10,... | collective-permute-start | bytes 1572872 | tf_op jit(solution)/shard_map/ppermute | solution.py:92
  34.1 220.0 %collective-permute-start.4 = (bf16[256,1024]{1,0:T(8,128)(2,1)}, bf16[256,1024]{1,0:T(8,128)(2,1)S(1)}, u32[]{:S(2)}, u32[]{:S(2)}) collective-permute-start(bf16[256,1024]{1,0:T(8,128)(2,1)} %get-tuple-element.20), channel_id=1, source_target_pairs={{0,3},{1,4},{2,5},{3,6},{4,7},{5,0},{6,1},{7,2},{8,11},{9,12},{10,... | collective-permute-start | bytes 1572872 | tf_op jit(solution)/shard_map/ppermute | solution.py:92
  40.5 4.6 %copy-start.4 = (s32[256]{0:T(256)S(1)}, s32[256]{0:T(256)}, u32[]{:S(2)}) copy-start(s32[256]{0:T(256)} %param.13) | copy-start | bytes 3076
  112.0 142.9 %collective-permute-start.5 = (bf16[256,1024]{1,0:T(8,128)(2,1)}, bf16[256,1024]{1,0:T(8,128)(2,1)S(1)}, u32[]{:S(2)}, u32[]{:S(2)}) collective-permute-start(bf16[256,1024]{1,0:T(8,128)(2,1)} %get-tuple-element.25), channel_id=1, source_target_pairs={{0,2},{1,3},{2,4},{3,5},{4,6},{5,7},{6,0},{7,1},{8,10},{9,11},{10,... | collective-permute-start | bytes 1572872 | tf_op jit(solution)/shard_map/ppermute | solution.py:92
  125.4 130.4 %collective-permute-start.6 = (bf16[256,1024]{1,0:T(8,128)(2,1)}, bf16[256,1024]{1,0:T(8,128)(2,1)S(1)}, u32[]{:S(2)}, u32[]{:S(2)}) collective-permute-start(bf16[256,1024]{1,0:T(8,128)(2,1)} %get-tuple-element.18), channel_id=1, source_target_pairs={{0,1},{1,2},{2,3},{3,4},{4,5},{5,6},{6,7},{7,0},{8,9},{9,10},{10,1... | collective-permute-start | bytes 1572872 | tf_op jit(solution)/shard_map/ppermute | solution.py:92
  274.4 19.1 %all-to-all-start.1 = ((bf16[32,8,1024]{2,1,0:T(8,128)(2,1)}), bf16[32,8,1024]{2,1,0:T(8,128)(2,1)S(1)}, u32[]{:S(2)}, u32[]{:S(2)}) async-start(bf16[32,8,1024]{2,1,0:T(8,128)(2,1)} %fusion.7), calls=%async_computation.1 | async-start | bytes 1048576 | tf_op jit(solution)/shard_map/all_to_all | solution.py:107
  277.2 105.1 %all-gather.4.cloned.1.call-start = ((), (), s32[]{:S(2)}) async-start(), calls=%async_computation.3 | async-start | bytes 4718592 | tf_op jit(solution)/shard_map/all_gather | solution.py:138
  390.3 28.6 %copy-start.3 = (bf16[1024,1024]{1,0:T(8,128)(2,1)}, bf16[1024,1024]{1,0:T(8,128)(2,1)S(1)}, u32[]{:S(2)}) copy-start(bf16[1024,1024]{1,0:T(8,128)(2,1)S(1)} %convolution_convert_fusion.2) | copy-start | bytes 6291460
  391.4 15.1 %collective-permute-start.9 = (bf16[256,1024]{1,0:T(8,128)(2,1)}, bf16[256,1024]{1,0:T(8,128)(2,1)}, u32[]{:S(2)}, u32[]{:S(2)}) collective-permute-start(bf16[256,1024]{1,0:T(8,128)(2,1)} %get-tuple-element.27), channel_id=1, source_target_pairs={{0,24},{8,0},{16,8},{24,16},{1,25},{9,1},{17,9},{25,17},{2,26},{10... | collective-permute-start | bytes 1572872 | tf_op jit(solution)/shard_map/ppermute | solution.py:151
  393.8 25.1 %collective-permute-start.8 = (bf16[256,1024]{1,0:T(8,128)(2,1)S(1)}, bf16[256,1024]{1,0:T(8,128)(2,1)}, u32[]{:S(2)}, u32[]{:S(2)}) collective-permute-start(bf16[256,1024]{1,0:T(8,128)(2,1)S(1)} %get-tuple-element.28), channel_id=1, source_target_pairs={{0,16},{8,24},{16,0},{24,8},{1,17},{9,25},{17,1},{25,9},{2,18},{10... | collective-permute-start | bytes 1572872 | tf_op jit(solution)/shard_map/ppermute | solution.py:151
  394.3 24.6 %collective-permute-start.7 = (bf16[256,1024]{1,0:T(8,128)(2,1)S(1)}, bf16[256,1024]{1,0:T(8,128)(2,1)}, u32[]{:S(2)}, u32[]{:S(2)}) collective-permute-start(bf16[256,1024]{1,0:T(8,128)(2,1)S(1)} %get-tuple-element.26), channel_id=1, source_target_pairs={{0,8},{8,16},{16,24},{24,0},{1,9},{9,17},{17,25},{25,1},{2,10},{10... | collective-permute-start | bytes 1572872 | tf_op jit(solution)/shard_map/ppermute | solution.py:151
  418.9 29.3 %copy-start.1 = (bf16[1024,1024]{1,0:T(8,128)(2,1)S(1)}, bf16[1024,1024]{1,0:T(8,128)(2,1)}, u32[]{:S(2)}) copy-start(bf16[1024,1024]{1,0:T(8,128)(2,1)} %param.15) | copy-start | bytes 6291460
  421.5 15.8 %collective-permute-start.10 = (bf16[256,1024]{1,0:T(8,128)(2,1)S(1)}, bf16[256,1024]{1,0:T(8,128)(2,1)S(1)}, u32[]{:S(2)}, u32[]{:S(2)}) collective-permute-start(bf16[256,1024]{1,0:T(8,128)(2,1)S(1)} %get-tuple-element.17), channel_id=1, source_target_pairs={{0,8},{8,16},{16,24},{24,0},{1,9},{9,17},{17,25},{25,1},{2,10},{10... | collective-permute-start | bytes 1572872 | tf_op jit(solution)/shard_map/ppermute | solution.py:157
  422.1 23.9 %collective-permute-start.11 = (bf16[256,1024]{1,0:T(8,128)(2,1)S(1)}, bf16[256,1024]{1,0:T(8,128)(2,1)S(1)}, u32[]{:S(2)}, u32[]{:S(2)}) collective-permute-start(bf16[256,1024]{1,0:T(8,128)(2,1)S(1)} %get-tuple-element.17), channel_id=1, source_target_pairs={{0,16},{8,24},{16,0},{24,8},{1,17},{9,25},{17,1},{25,9},{2,18},{10... | collective-permute-start | bytes 1572872 | tf_op jit(solution)/shard_map/ppermute | solution.py:157
  422.7 23.4 %collective-permute-start.12 = (bf16[256,1024]{1,0:T(8,128)(2,1)S(1)}, bf16[256,1024]{1,0:T(8,128)(2,1)S(1)}, u32[]{:S(2)}, u32[]{:S(2)}) collective-permute-start(bf16[256,1024]{1,0:T(8,128)(2,1)S(1)} %get-tuple-element.17), channel_id=1, source_target_pairs={{0,24},{8,0},{16,8},{24,16},{1,25},{9,1},{17,9},{25,17},{2,26},{10... | collective-permute-start | bytes 1572872 | tf_op jit(solution)/shard_map/ppermute | solution.py:157
  446.2 2.0 copy-start.2
Sparse Core Ops, SparseCore 0:
  11.6 230.9 all-gather.5
  337.4 44.7 all-gather.3

commit v3 on v2

--- a/solution.py
+++ b/solution.py
@@ -80,7 +80,6 @@
     capacity = token_count // device_count
     everyone = ("dp", "fsdp")
     low = states.dtype
-    share = value_matrix.shape[0] // group_dp
     block = model_width // group_fsdp
     me = lax.axis_index("fsdp")
     blocks = []
@@ -91,8 +90,13 @@
             pairs = [(i, (i + step) % group_fsdp) for i in range(group_fsdp)]
             piece = lax.ppermute(piece, "fsdp", pairs)
         blocks.append(piece)
-    own_share = lax.dynamic_slice_in_dim(value_matrix, lax.axis_index("dp") * share, share, 0)
-    whole = lax.all_gather(own_share, everyone, axis=0)
+    back = [blocks[-t % group_fsdp] for t in range(group_fsdp)]
+    first = lax.rem(group_fsdp - me, group_fsdp) * token_count
+    column_states = lax.dynamic_slice_in_dim(
+        jnp.concatenate(back + back[:-1], axis=0), first, group_fsdp * token_count, 0
+    )
+    partial = jnp.dot(column_states, value_matrix, preferred_element_type=jnp.float32).astype(low)
+    values = lax.psum_scatter(partial, "fsdp", scatter_dimension=0, tiled=True)
 
     row = jnp.arange(token_count, dtype=jnp.int32)
     earlier = (dest_device[:, None] == dest_device[None, :]) & (row[None, :] < row[:, None])
@@ -114,9 +118,6 @@
         return moved.reshape(token_count, width)
 
     got = exchange(ordered_dot(pack, joined))
-    turned = states.reshape(token_count, group_fsdp, group_dp, share).transpose(0, 2, 1, 3)
-    turned = turned.reshape(token_count, model_width)
-    values = jnp.dot(turned, whole.reshape(model_width, -1), preferred_element_type=jnp.float32).astype(low)
     got_values = exchange(ordered_dot(pack, values))
     target = got[:, -128].astype(jnp.int32)
     place = (target[None, :] == row[:, None]).astype(low)
@@ -127,12 +128,6 @@
     attention_fn, query_gradient, key_gradient, value_gradient = attend_block(
         learner_queries, learner_keys, ordered_dot(place, got_values), response_numbers, cotangent
     )
-    back = [blocks[-t % group_fsdp] for t in range(group_fsdp)]
-    first = lax.rem(group_fsdp - me, group_fsdp) * token_count
-    column_states = lax.dynamic_slice_in_dim(
-        jnp.concatenate(back + back[:-1], axis=0), first, group_fsdp * token_count, 0
-    )
-    value_gradient, column_states = lax.optimization_barrier((value_gradient, column_states))
     returned = exchange(ordered_dot(place.T, value_gradient))
     row_grads = ordered_dot(pack.T, returned)
     group_grads = lax.all_gather(row_grads, "fsdp", axis=0, tiled=True)

time: 456 us -> 422 us (0.925)
  starting transfers between devices: 82.1 us -> 27.9 us
  waiting for transfers between devices: 240 us -> 275 us
  local copies, waits for them, and re-layouts: 41.8 us -> 31.4 us
    reduce_scatter x0 -> x1, waiting for transfers between devices: none -> 81 us  [per_device(): values = lax.psum_scatter(partial, 'fsdp', scatter_dimension=0, tiled=True)]
    ppermute x7, waiting for transfers between devices: 147 us -> 84.4 us  [per_device(): piece = lax.ppermute(piece, 'fsdp', pairs)]
    ppermute x7, starting transfers between devices: 64.7 us -> 7.82 us  [per_device(): piece = lax.ppermute(piece, 'fsdp', pairs)]
    all_to_all x2, waiting for transfers between devices: 3.76 us -> 21.4 us  [exchange(): lax.all_to_all(rows.reshape(device_count, capacity, width), everyone, spl...]
    dot_general x6, matrix products: 23 us -> 12.6 us  [ordered_dot(): jnp.dot(one_hot, rows, preferred_element_type=jnp.float32)]
    dot_general x0 -> x1, matrix products: none -> 8.31 us  [per_device(): jnp.dot(column_states, value_matrix, preferred_element_type=jnp.float32)]
    dynamic_slice x2 -> x0, local copies, waits for them, and re-layouts: 5.47 us -> none  [the longest x1 4.64 us: per_device(): lax.dynamic_slice_in_dim(jnp.concatenate(back + back[:-1], axis=0), first...]
    transpose x1 -> x0, local copies, waits for them, and re-layouts: 4.61 us -> none  [per_device(): states.reshape(token_count, group_fsdp, group_dp, share)]
  transfers between devices with their start and end apart: 17 -> 17, of which waited for: 9 -> 14; matrix products, arithmetic and copies ran while one was open for 13% -> 5% of each run, Pallas kernels for 0% -> 0%
where the time goes in v3:
time: 422 us; the launch traced here: 421 us
  waiting for transfers between devices  275 us (65%)
  local copies, waits for them, and re-layouts  31.4 us (7%)
  matrix products  28.9 us (7%)
  starting transfers between devices  27.9 us (7%)
  Pallas kernels  21.8 us (5%)
  blocking collectives  18.4 us (4%)
  between operations  14.3 us (3%)
    ppermute x7, waiting for transfers between devices, per_device(): piece = lax.ppermute(piece, 'fsdp', pairs)  84.4 us
    reduce_scatter x1, waiting for transfers between devices, per_device(): values = lax.psum_scatter(partial, 'fsdp', scatter_dimension=0, tiled=True)  81 us
    all_gather x1, waiting for transfers between devices, per_device(): group_grads = lax.all_gather(row_grads, 'fsdp', axis=0, tiled=True)  44.9 us
    ppermute x3, waiting for transfers between devices, per_device(): sent.append(lax.ppermute(piece, 'dp', rings[step]))  22.2 us
    pallas_call x1, Pallas kernels, attend_block(): pl.pallas_call(attend_kernel, grid=(KEY_VALUE_HEADS,), in_specs=[wide, th...  21.8 us
    unnamed x27, local copies, waits for them, and re-layouts  21.4 us
    all_to_all x2, waiting for transfers between devices, exchange(): lax.all_to_all(rows.reshape(device_count, capacity, width), everyone, spl...  21.4 us
    ppermute x3, waiting for transfers between devices, per_device(): piece = lax.ppermute(summed, 'dp', rings[step]) if step else summed  21.4 us
  transfers between devices with their start and end apart: 17, of which 14 were waited for; matrix products, arithmetic and copies ran while one was open for 5% of the time, Pallas kernels for 0%

profile of v3, /device:TPU:0, one launch (start us, length us, event | category | flops | bytes accessed | tf_op | source)
XLA Modules:
  0.0 421.5 jit_solution(11275147531736645018)
XLA Ops:
  7.3 4.3 %constant_dynamic-slice_fusion.3 = (bf16[256,1024]{1,0:T(8,128)(2,1)}, bf16[3840,1024]{1,0:T(8,128)(2,1)}, bf16[256,1024]{1,0:T(8,128)(2,1)}, bf16[256,1024]{1,0...) fusion(bf16[256,8192]{1,0:T(8,128)(2,1)} %param.8, ...), kind=kLoop, calls=%fused_computation.58 | loop fusion | bytes 8388640 | tf_op jit(solution)/shard_map/dynamic_slice | solution.py:88
  11.6 4.5 %collective-permute-start = (bf16[256,1024]{1,0:T(8,128)(2,1)}, bf16[256,1024]{1,0:T(8,128)(2,1)S(1)}, u32[]{:S(2)}, u32[]{:S(2)}) collective-permute-start(bf16[256,1024]{1,0:T(8,128)(2,1)} %get-tuple-element.20), channel_id=1, source_target_pairs={{0,7},{1,0},{2,1},{3,2},{4,3},{5,4},{6,5},{7,6},{8,15},{9,8},{10,9... | collective-permute-start | bytes 1572872 | tf_op jit(solution)/shard_map/ppermute | solution.py:91
  16.7 2.7 collective-permute-start.3
  19.4 9.3 %collective-permute-done = bf16[256,1024]{1,0:T(8,128)(2,1)S(1)} collective-permute-done((bf16[256,1024]{1,0:T(8,128)(2,1)}, bf16[256,1024]{1,0:T(8,128)(2,1)S(1)}, u32[]{:S(2)}, u32[]{:S(2)}) %collective-permute-start) | collective-permute-done | bytes 524320 | tf_op jit(solution)/shard_map/ppermute | solution.py:91
  29.6 10.4 %collective-permute-done.1 = bf16[256,1024]{1,0:T(8,128)(2,1)S(1)} collective-permute-done((bf16[256,1024]{1,0:T(8,128)(2,1)}, bf16[256,1024]{1,0:T(8,128)(2,1)S(1)}, u32[]{:S(2)}, u32[]{:S(2)}) %collective-permute-start.1) | collective-permute-done | bytes 524320 | tf_op jit(solution)/shard_map/ppermute | solution.py:91
  40.8 10.4 %collective-permute-done.2 = bf16[256,1024]{1,0:T(8,128)(2,1)} collective-permute-done((bf16[256,1024]{1,0:T(8,128)(2,1)}, bf16[256,1024]{1,0:T(8,128)(2,1)}, u32[]{:S(2)}, u32[]{:S(2)}) %collective-permute-start.2) | collective-permute-done | bytes 524320 | tf_op jit(solution)/shard_map/ppermute | solution.py:91
  53.1 54.3 %collective-permute-done.3 = bf16[256,1024]{1,0:T(8,128)(2,1)} collective-permute-done((bf16[256,1024]{1,0:T(8,128)(2,1)}, bf16[256,1024]{1,0:T(8,128)(2,1)}, u32[]{:S(2)}, u32[]{:S(2)}) %collective-permute-start.3) | collective-permute-done | bytes 524320 | tf_op jit(solution)/shard_map/ppermute | solution.py:91
  122.8 8.3 %convolution_convert_fusion.2 = bf16[2048,1024]{1,0:T(8,128)(2,1)} fusion(bf16[1024,1024]{1,0:T(8,128)(2,1)S(1)} %copy-done, bf16[3840,1024]{1,0:T(8,128)(2,1)} %constant_dynamic-update-slice_fusion, s32[]{:T(128)S(6)} %select_n.53), kind=kOutput, calls=%fused_computation.3 | convolution fusion | flops 4297064448 | bytes 10485764 | tf_op jit(solution)/shard_map/dot_general | solution.py:98
  131.5 4.1 fusion
  135.5 3.7 all-to-all-start
  139.2 81.0 %reduce-scatter.2.cloned.1.call-done = bf16[256,1024]{1,0:T(8,128)(2,1)} async-done(((bf16[2048,1024]{1,0:T(8,128)(2,1)}), bf16[256,1024]{1,0:T(8,128)(2,1)}) %reduce-scatter.2.cloned.1.call-update) | async-done | bytes 524304 | tf_op jit(solution)/shard_map/reduce_scatter | solution.py:99
  222.4 12.0 %all-to-all-done = bf16[32,8,5248]{2,1,0:T(8,128)(2,1)} async-done(((bf16[32,8,5248]{2,1,0:T(8,128)(2,1)}), bf16[32,8,5248]{2,1,0:T(8,128)(2,1)}, u32[]{:S(2)}, u32[]{:S(2)}) %all-to-all-start) | async-done | bytes 2687008 | tf_op jit(solution)/shard_map/all_to_all | solution.py:111
  234.4 7.5 %all-to-all-start.1 = ((bf16[32,8,1024]{2,1,0:T(8,128)(2,1)}), bf16[32,8,1024]{2,1,0:T(8,128)(2,1)S(1)}, u32[]{:S(2)}, u32[]{:S(2)}) async-start(bf16[32,8,1024]{2,1,0:T(8,128)(2,1)} %fusion.12), calls=%async_computation.2 | async-start | bytes 1048576 | tf_op jit(solution)/shard_map/all_to_all | solution.py:111
  243.7 2.6 convolution_convert_fusion
  248.9 9.4 %all-to-all-done.1 = bf16[32,8,1024]{2,1,0:T(8,128)(2,1)S(1)} async-done(((bf16[32,8,1024]{2,1,0:T(8,128)(2,1)}), bf16[32,8,1024]{2,1,0:T(8,128)(2,1)S(1)}, u32[]{:S(2)}, u32[]{:S(2)}) %all-to-all-start.1) | async-done | bytes 524320 | tf_op jit(solution)/shard_map/all_to_all | solution.py:111
  259.5 21.8 %shard_map.111 = (bf16[256,4096]{1,0:T(8,128)(2,1)}, bf16[256,4096]{1,0:T(8,128)(2,1)}, bf16[256,1024]{1,0:T(8,128)(2,1)}, bf16[256,1024]{1,0:T(8,128)(2,1)}) custom-call(bf16[256,4096]{1,0:T(8,128)(2,1)} %slice.13.q_ref, bf16[256,1024]{1,0:T(8,128)(2,1)} %slice.14.k_ref, bf16[256,1024]{1,0:T(8,128)(2,1)} %convolution_convert_fusion.5.v_ref, ...), custom_call_target="tpu_custom_call" | custom-call | flops 3221225472 | bytes 10485760 | tf_op jit(solution)/shard_map/pallas_call | solution.py:55
  282.6 18.4 %all_to_all.15 = bf16[32,8,1024]{2,1,0:T(8,128)(2,1)S(1)} all-to-all(bf16[32,8,1024]{2,1,0:T(8,128)(2,1)S(1)} %fusion.13), channel_id=1, replica_groups=mesh['dp'=4,'fsdp'=8] {'dp','fsdp'}, dimensions={0} | all-to-all | bytes 1048576 | tf_op jit(solution)/shard_map/all_to_all | solution.py:111
  302.2 44.9 %all-gather.2.cloned.1.call-done = bf16[2048,1024]{1,0:T(8,128)(2,1)} async-done(((bf16[256,1024]{1,0:T(8,128)(2,1)}), bf16[2048,1024]{1,0:T(8,128)(2,1)}) %all-gather.2.cloned.1.call-update) | async-done | bytes 4194320 | tf_op jit(solution)/shard_map/all_gather | solution.py:133
  347.1 8.0 %fusion.9 = bf16[1024,1024]{1,0:T(8,128)(2,1)S(1)} fusion(bf16[2048,1024]{1,0:T(8,128)(2,1)} %all-gather.2.cloned.1.call-done, bf16[3840,1024]{1,0:T(8,128)(2,1)} %constant_dynamic-update-slice_fusion, s32[]{:T(128)S(6)} %select_n.53), kind=kOutput, calls=%fused_computation.12 | convolution fusion | flops 4296015872 | bytes 10485764 | tf_op jit(solution)/shard_map/dot_general | solution.py:134
  361.8 11.6 %collective-permute-done.7 = bf16[256,1024]{1,0:T(8,128)(2,1)} collective-permute-done((bf16[256,1024]{1,0:T(8,128)(2,1)}, bf16[256,1024]{1,0:T(8,128)(2,1)}, u32[]{:S(2)}, u32[]{:S(2)}) %collective-permute-start.7) | collective-permute-done | bytes 524320 | tf_op jit(solution)/shard_map/ppermute | solution.py:146
  373.4 10.5 %collective-permute-done.8 = bf16[256,1024]{1,0:T(8,128)(2,1)} collective-permute-done((bf16[256,1024]{1,0:T(8,128)(2,1)S(1)}, bf16[256,1024]{1,0:T(8,128)(2,1)}, u32[]{:S(2)}, u32[]{:S(2)}) %collective-permute-start.8) | collective-permute-done | bytes 524320 | tf_op jit(solution)/shard_map/ppermute | solution.py:146
  388.5 2.3 collective-permute-start.12
  390.8 11.4 %collective-permute-done.10 = bf16[256,1024]{1,0:T(8,128)(2,1)S(1)} collective-permute-done((bf16[256,1024]{1,0:T(8,128)(2,1)S(1)}, bf16[256,1024]{1,0:T(8,128)(2,1)S(1)}, u32[]{:S(2)}, u32[]{:S(2)}) %collective-permute-start.10) | collective-permute-done | bytes 524320 | tf_op jit(solution)/shard_map/ppermute | solution.py:152
  402.3 9.8 %collective-permute-done.11 = bf16[256,1024]{1,0:T(8,128)(2,1)S(1)} collective-permute-done((bf16[256,1024]{1,0:T(8,128)(2,1)S(1)}, bf16[256,1024]{1,0:T(8,128)(2,1)S(1)}, u32[]{:S(2)}, u32[]{:S(2)}) %collective-permute-start.11) | collective-permute-done | bytes 524320 | tf_op jit(solution)/shard_map/ppermute | solution.py:152
  (65 shorter events, 43.9 us)
Async XLA Ops:
  7.2 115.6 %copy-start = (bf16[1024,1024]{1,0:T(8,128)(2,1)S(1)}, bf16[1024,1024]{1,0:T(8,128)(2,1)}, u32[]{:S(2)}) copy-start(bf16[1024,1024]{1,0:T(8,128)(2,1)} %param.15) | copy-start | bytes 6291460
  7.2 213.1 %reduce-scatter.2.cloned.1.call-start = ((), (), s32[]{:S(2)}) async-start(), calls=%async_computation.4 | async-start | bytes 4718592 | tf_op jit(solution)/shard_map/reduce_scatter | solution.py:99
  11.6 17.1 %collective-permute-start = (bf16[256,1024]{1,0:T(8,128)(2,1)}, bf16[256,1024]{1,0:T(8,128)(2,1)S(1)}, u32[]{:S(2)}, u32[]{:S(2)}) collective-permute-start(bf16[256,1024]{1,0:T(8,128)(2,1)} %get-tuple-element.20), channel_id=1, source_target_pairs={{0,7},{1,0},{2,1},{3,2},{4,3},{5,4},{6,5},{7,6},{8,15},{9,8},{10,9... | collective-permute-start | bytes 1572872 | tf_op jit(solution)/shard_map/ppermute | solution.py:91
  16.1 23.9 %collective-permute-start.1 = (bf16[256,1024]{1,0:T(8,128)(2,1)}, bf16[256,1024]{1,0:T(8,128)(2,1)S(1)}, u32[]{:S(2)}, u32[]{:S(2)}) collective-permute-start(bf16[256,1024]{1,0:T(8,128)(2,1)} %get-tuple-element.19), channel_id=1, source_target_pairs={{0,6},{1,7},{2,0},{3,1},{4,2},{5,3},{6,4},{7,5},{8,14},{9,15},{10,... | collective-permute-start | bytes 1572872 | tf_op jit(solution)/shard_map/ppermute | solution.py:91
  16.7 34.5 %collective-permute-start.2 = (bf16[256,1024]{1,0:T(8,128)(2,1)}, bf16[256,1024]{1,0:T(8,128)(2,1)}, u32[]{:S(2)}, u32[]{:S(2)}) collective-permute-start(bf16[256,1024]{1,0:T(8,128)(2,1)} %get-tuple-element.18), channel_id=1, source_target_pairs={{0,5},{1,6},{2,7},{3,0},{4,1},{5,2},{6,3},{7,4},{8,13},{9,14},{10,... | collective-permute-start | bytes 1572872 | tf_op jit(solution)/shard_map/ppermute | solution.py:91
  16.7 90.7 %collective-permute-start.3 = (bf16[256,1024]{1,0:T(8,128)(2,1)}, bf16[256,1024]{1,0:T(8,128)(2,1)}, u32[]{:S(2)}, u32[]{:S(2)}) collective-permute-start(bf16[256,1024]{1,0:T(8,128)(2,1)} %get-tuple-element.17), channel_id=1, source_target_pairs={{0,4},{1,5},{2,6},{3,7},{4,0},{5,1},{6,2},{7,3},{8,12},{9,13},{10,... | collective-permute-start | bytes 1572872 | tf_op jit(solution)/shard_map/ppermute | solution.py:91
  19.4 89.8 %collective-permute-start.4 = (bf16[256,1024]{1,0:T(8,128)(2,1)}, bf16[256,1024]{1,0:T(8,128)(2,1)}, u32[]{:S(2)}, u32[]{:S(2)}) collective-permute-start(bf16[256,1024]{1,0:T(8,128)(2,1)} %get-tuple-element.16), channel_id=1, source_target_pairs={{0,3},{1,4},{2,5},{3,6},{4,7},{5,0},{6,1},{7,2},{8,11},{9,12},{10,... | collective-permute-start | bytes 1572872 | tf_op jit(solution)/shard_map/ppermute | solution.py:91
  28.7 82.4 %collective-permute-start.5 = (bf16[256,1024]{1,0:T(8,128)(2,1)}, bf16[256,1024]{1,0:T(8,128)(2,1)S(1)}, u32[]{:S(2)}, u32[]{:S(2)}) collective-permute-start(bf16[256,1024]{1,0:T(8,128)(2,1)} %get-tuple-element.21), channel_id=1, source_target_pairs={{0,2},{1,3},{2,4},{3,5},{4,6},{5,7},{6,0},{7,1},{8,10},{9,11},{10,... | collective-permute-start | bytes 1572872 | tf_op jit(solution)/shard_map/ppermute | solution.py:91
  40.0 72.0 %collective-permute-start.6 = (bf16[256,1024]{1,0:T(8,128)(2,1)}, bf16[256,1024]{1,0:T(8,128)(2,1)S(1)}, u32[]{:S(2)}, u32[]{:S(2)}) collective-permute-start(bf16[256,1024]{1,0:T(8,128)(2,1)} %get-tuple-element.14), channel_id=1, source_target_pairs={{0,1},{1,2},{2,3},{3,4},{4,5},{5,6},{6,7},{7,0},{8,9},{9,10},{10,1... | collective-permute-start | bytes 1572872 | tf_op jit(solution)/shard_map/ppermute | solution.py:91
  122.8 8.4 %copy-start.6 = (s32[256]{0:T(256)S(1)}, s32[256]{0:T(256)}, u32[]{:S(2)}) copy-start(s32[256]{0:T(256)} %param.12) | copy-start | bytes 3076
  122.8 8.4 %copy-start.3 = (s32[256]{0:T(256)S(1)}, s32[256]{0:T(256)}, u32[]{:S(2)}) copy-start(s32[256]{0:T(256)} %param.11) | copy-start | bytes 3076
  122.8 8.7 %copy-start.5 = (bf16[256,1024]{1,0:T(8,128)(2,1)S(1)}, bf16[256,1024]{1,0:T(8,128)(2,1)}, u32[]{:S(2)}) copy-start(bf16[256,1024]{1,0:T(8,128)(2,1)} %param.10) | copy-start | bytes 1572868
  135.5 106.4 %copy-start.4 = (s32[256]{0:T(256)S(1)}, s32[256]{0:T(256)}, u32[]{:S(2)}) copy-start(s32[256]{0:T(256)} %param.13) | copy-start | bytes 3076
  135.5 98.8 %all-to-all-start = ((bf16[32,8,5248]{2,1,0:T(8,128)(2,1)}), bf16[32,8,5248]{2,1,0:T(8,128)(2,1)}, u32[]{:S(2)}, u32[]{:S(2)}) async-start(bf16[32,8,5248]{2,1,0:T(8,128)(2,1)} %fusion), calls=%async_computation | async-start | bytes 5373952 | tf_op jit(solution)/shard_map/all_to_all | solution.py:111
  234.4 23.9 %all-to-all-start.1 = ((bf16[32,8,1024]{2,1,0:T(8,128)(2,1)}), bf16[32,8,1024]{2,1,0:T(8,128)(2,1)S(1)}, u32[]{:S(2)}, u32[]{:S(2)}) async-start(bf16[32,8,1024]{2,1,0:T(8,128)(2,1)} %fusion.12), calls=%async_computation.2 | async-start | bytes 1048576 | tf_op jit(solution)/shard_map/all_to_all | solution.py:111
  241.9 105.2 %all-gather.2.cloned.1.call-start = ((), (), s32[]{:S(2)}) async-start(), calls=%async_computation.5 | async-start | bytes 4718592 | tf_op jit(solution)/shard_map/all_gather | solution.py:133
  355.1 1.3 copy-start.2
  357.4 16.0 %collective-permute-start.7 = (bf16[256,1024]{1,0:T(8,128)(2,1)}, bf16[256,1024]{1,0:T(8,128)(2,1)}, u32[]{:S(2)}, u32[]{:S(2)}) collective-permute-start(bf16[256,1024]{1,0:T(8,128)(2,1)} %get-tuple-element.22), channel_id=1, source_target_pairs={{0,8},{8,16},{16,24},{24,0},{1,9},{9,17},{17,25},{25,1},{2,10},{10... | collective-permute-start | bytes 1572872 | tf_op jit(solution)/shard_map/ppermute | solution.py:146
  358.9 25.0 %collective-permute-start.8 = (bf16[256,1024]{1,0:T(8,128)(2,1)S(1)}, bf16[256,1024]{1,0:T(8,128)(2,1)}, u32[]{:S(2)}, u32[]{:S(2)}) collective-permute-start(bf16[256,1024]{1,0:T(8,128)(2,1)S(1)} %get-tuple-element.24), channel_id=1, source_target_pairs={{0,16},{8,24},{16,0},{24,8},{1,17},{9,25},{17,1},{25,9},{2,18},{10... | collective-permute-start | bytes 1572872 | tf_op jit(solution)/shard_map/ppermute | solution.py:146
  360.3 23.6 %collective-permute-start.9 = (bf16[256,1024]{1,0:T(8,128)(2,1)S(1)}, bf16[256,1024]{1,0:T(8,128)(2,1)}, u32[]{:S(2)}, u32[]{:S(2)}) collective-permute-start(bf16[256,1024]{1,0:T(8,128)(2,1)S(1)} %get-tuple-element.23), channel_id=1, source_target_pairs={{0,24},{8,0},{16,8},{24,16},{1,25},{9,1},{17,9},{25,17},{2,26},{10... | collective-permute-start | bytes 1572872 | tf_op jit(solution)/shard_map/ppermute | solution.py:146
  386.4 15.8 %collective-permute-start.10 = (bf16[256,1024]{1,0:T(8,128)(2,1)S(1)}, bf16[256,1024]{1,0:T(8,128)(2,1)S(1)}, u32[]{:S(2)}, u32[]{:S(2)}) collective-permute-start(bf16[256,1024]{1,0:T(8,128)(2,1)S(1)} %get-tuple-element.13), channel_id=1, source_target_pairs={{0,8},{8,16},{16,24},{24,0},{1,9},{9,17},{17,25},{25,1},{2,10},{10... | collective-permute-start | bytes 1572872 | tf_op jit(solution)/shard_map/ppermute | solution.py:152
  388.0 24.1 %collective-permute-start.11 = (bf16[256,1024]{1,0:T(8,128)(2,1)S(1)}, bf16[256,1024]{1,0:T(8,128)(2,1)S(1)}, u32[]{:S(2)}, u32[]{:S(2)}) collective-permute-start(bf16[256,1024]{1,0:T(8,128)(2,1)S(1)} %get-tuple-element.13), channel_id=1, source_target_pairs={{0,16},{8,24},{16,0},{24,8},{1,17},{9,25},{17,1},{25,9},{2,18},{10... | collective-permute-start | bytes 1572872 | tf_op jit(solution)/shard_map/ppermute | solution.py:152
  388.5 23.9 %collective-permute-start.12 = (bf16[256,1024]{1,0:T(8,128)(2,1)S(1)}, bf16[256,1024]{1,0:T(8,128)(2,1)S(1)}, u32[]{:S(2)}, u32[]{:S(2)}) collective-permute-start(bf16[256,1024]{1,0:T(8,128)(2,1)S(1)} %get-tuple-element.13), channel_id=1, source_target_pairs={{0,24},{8,0},{16,8},{24,16},{1,25},{9,1},{17,9},{25,17},{2,26},{10... | collective-permute-start | bytes 1572872 | tf_op jit(solution)/shard_map/ppermute | solution.py:152
  412.6 2.0 copy-start.1
Sparse Core Ops, SparseCore 0:
  131.2 88.9 reduce-scatter.1
  302.3 44.7 all-gather.1
